TPU v7x, 1024 devices: a whole 8x8x8 slice. The times are simulated.
1024 devices in a mesh: pipe: 16 (over y, core), expert: 64 (over z, x).
Axes of the slice: x: 8, y: 8, z: 8, core: 2. Of those that a mesh axis runs over, the one named last changes fastest.
Arguments:
- tokens: bfloat16 [8192, 3584], P('expert', 'pipe'), may hold values from -170 to 170
- routes: int32 [8192, 2], P('expert'), may hold values from 0 to 63, all different within a row; in each aligned block of 128 rows (0 to 127, 128 to 255, ...) at most 5 rows name the same one
- router: bfloat16 [3584, 64], P('pipe'), may hold values from -0.09375 to 0.09375
- w_gate: bfloat16 [64, 3584, 2048], P('expert', None, 'pipe'), may hold values from -0.09375 to 0.09375
- w_up: bfloat16 [64, 3584, 2048], P('expert', None, 'pipe'), may hold values from -0.09375 to 0.09375
- w_down: bfloat16 [64, 2048, 3584], P('expert', 'pipe'), may hold values from -0.125 to 0.125
Outputs:
- mixed: bfloat16 [8192, 3584], P('expert', 'pipe')
Inputs may be any that keep to these rules, and one draw needn't show every extreme that they name: `routes`: each row names 2 different experts; among the 128 rows of one index of expert no expert is named more than 5 times.
All inputs are finite; a program needn't handle non-finite values.
Results may differ from a plain program's by a relative error of at most 0.024.
Values may be sent and summed in bfloat16 or wider, within the bound.
A program may use at most 32 MiB of HBM per device.

v0:
```python
import jax
import jax.numpy as jnp
from jax import lax
from jax.sharding import PartitionSpec as P

eps = 1e-06


def body(tokens, routes, router, w_gate, w_up, w_down):
    tok_rows, part_width = tokens.shape
    experts = router.shape[1]
    topk = routes.shape[1]
    capacity = max(2, tok_rows * topk // experts + max(1, tok_rows * topk // (4 * experts)))
    blocks = lax.axis_size("pipe")
    width = part_width * blocks
    xf = tokens.astype(jnp.float32)
    part_square = jnp.sum(xf * xf, axis=1)
    part_logits = jnp.dot(tokens, router, preferred_element_type=jnp.float32)
    square_sum, logits = lax.psum((part_square, part_logits), "pipe")
    rstd = lax.rsqrt(square_sum / width + eps)
    logits = rstd[:, None] * logits
    score = jax.nn.sigmoid(jnp.take_along_axis(logits, routes, axis=1))
    weight = score / jnp.sum(score, axis=1, keepdims=True)
    flat_routes = routes.reshape(-1)
    onehot = (flat_routes[:, None] == jnp.arange(experts, dtype=jnp.int32)[None, :]).astype(
        jnp.int32
    )
    position = jnp.cumsum(onehot, axis=0) - 1
    slot = jnp.take_along_axis(position, flat_routes[:, None], axis=1)[:, 0]
    dest = flat_routes * capacity + slot
    token_of = jnp.arange(tok_rows * topk, dtype=jnp.int32) // topk
    outgoing = (
        jnp.zeros((experts * capacity, part_width), jnp.bfloat16).at[dest].set(tokens[token_of])
    )
    incoming = lax.all_to_all(
        outgoing.reshape(experts, capacity, part_width),
        "expert",
        split_axis=0,
        concat_axis=0,
        tiled=True,
    )
    rows = incoming.reshape(experts * capacity, part_width)
    gate_weight = w_gate[0]
    up_weight = w_up[0]
    piece = lax.all_gather(rows, "pipe", axis=1, tiled=True)
    gate_acc = jnp.dot(piece, gate_weight, preferred_element_type=jnp.float32)
    up_acc = jnp.dot(piece, up_weight, preferred_element_type=jnp.float32)
    piece_float = piece.astype(jnp.float32)
    square_acc = jnp.sum(piece_float * piece_float, axis=1)
    gate_acc, up_acc, square_acc = (gate_acc, up_acc, square_acc)
    row_scale = lax.rsqrt(square_acc / width + eps)[:, None]
    hidden = (jax.nn.silu(row_scale * gate_acc) * (row_scale * up_acc)).astype(jnp.bfloat16)
    down_weight = w_down[0]
    summed = (
        lax.psum_scatter(
            jnp.einsum("fc,rf->cr", down_weight, hidden, preferred_element_type=jnp.float32).astype(
                jnp.bfloat16
            ),
            "pipe",
            scatter_dimension=0,
            tiled=True,
        )
        .astype(jnp.float32)
        .T
    )
    expert_out = summed.astype(jnp.bfloat16).reshape(experts, capacity, part_width)
    returned = lax.all_to_all(expert_out, "expert", split_axis=0, concat_axis=0, tiled=True)
    picked = returned.reshape(experts * capacity, part_width)[dest]
    picked = picked.reshape(tok_rows, topk, part_width).astype(jnp.float32)
    mixed = jnp.sum(weight[:, :, None] * picked, axis=1)
    return mixed.astype(jnp.bfloat16)


def solution(mesh):
    placed = (
        P("expert", "pipe"),
        P("expert", None),
        P("pipe", None),
        P("expert", None, "pipe"),
        P("expert", None, "pipe"),
        P("expert", "pipe", None),
    )
    return jax.shard_map(
        body, mesh=mesh, in_specs=placed, out_specs=P("expert", "pipe"), check_vma=False
    )
```

profile of v0, /device:TPU:1, one launch (start us, length us, event | category | flops | bytes accessed | tf_op | source)
XLA Modules:
  0.0 213.0 jit_solution(18223549678953282515)
XLA Ops:
  6.5 0.9 copy.35
  7.4 0.1 eq.17
  7.5 0.1 broadcast_in_dim_reshape.4
  7.7 0.1 reshape.262
  7.9 0.6 reduce-window.6
  8.5 0.2 slice_reduce_fusion
  8.9 0.9 copy.39
  9.8 2.4 %gather_fusion.2 = s32[256]{0:T(256)S(1)} fusion(s32[256,64]{0,1:T(8,128)S(1)} %bitcast_bitcast_fusion, s32[256]{0:T(256)S(1)} %bitcast.40), kind=kCustom, calls=%fused_computation.3 | custom fusion | bytes 4096 | tf_op jit(solution)/shard_map/jit(take_along_axis)/gather | solution.py:29
  12.2 2.2 %scatter_custom_fusion = bf16[320,224]{1,0:T(8,128)(2,1)S(1)} fusion(s32[256]{0:T(256)S(1)} %bitcast.43, bf16[128,224]{1,0:T(8,128)(2,1)S(1)} %copy.39, s32[1024]{0:T(1024)S(1)} %pad_clamp_fusion.1, bf16[]{:T(256)} %constant.65.clone.1), kind=kCustom, calls=%fused_computation.21 | custom fusion | bytes 143362 | tf_op jit(solution)/shard_map/scatter | solution.py:33
  14.5 35.6 %all_to_all.10 = bf16[64,5,224]{2,1,0:T(8,128)(2,1)S(1)} all-to-all(bf16[64,5,224]{2,1,0:T(8,128)(2,1)S(1)} %reshape.264), channel_id=1, replica_groups=mesh['pipe'=16,'expert'=64] {'expert'}, dimensions={0} | all-to-all | bytes 286720 | tf_op jit(solution)/shard_map/all_to_all | solution.py:35
  50.1 0.8 reshape.265
  51.0 41.4 %all-gather.3.cloned.1.call-done = bf16[16,224,320]{1,2,0:T(8,128)(2,1)} async-done(((bf16[1,224,320]{1,2,0:T(8,128)(2,1)}), bf16[16,224,320]{1,2,0:T(8,128)(2,1)}) %all-gather.3.cloned.1.call-update) | async-done | bytes 2293776 | tf_op jit(solution)/shard_map/all_gather | solution.py:45
  92.4 4.7 %copy.40 = bf16[16,224,320]{1,0,2:T(8,128)(2,1)} copy(bf16[16,224,320]{1,2,0:T(8,128)(2,1)} %all-gather.3.cloned.1.call-done) | data formatting | bytes 4587520 | tf_op jit(solution)/shard_map/all_gather | solution.py:45
  97.1 5.2 %reshape.313 = bf16[3584,320]{0,1:T(8,128)(2,1)S(1)} reshape(bf16[16,224,320]{1,0,2:T(8,128)(2,1)} %copy.40) | data formatting | bytes 4587520
  102.3 0.5 multiply_reduce_fusion
  102.9 0.6 copy-done.1
  103.5 0.8 convolution_multiply_fusion.1
  104.2 5.1 %fusion = bf16[3584,320]{0,1:T(8,128)(2,1)} fusion(bf16[3584,320]{0,1:T(8,128)(2,1)S(1)} %reshape.313, bf16[1,128,3584]{2,1,0:T(8,128)(2,1)S(1)} %copy-done, bf16[1,3584,128]{2,1,0:T(8,128)(2,1)} %param.10, f32[320,128]{1,0:T(8,128)S(1)} %convolution_multiply_fusion.1, f32[320]{0:T(512)S(1)} %add_rsqrt_fusion), kind=kOutput, calls=%fused_computation.6 | convolution fusion | flops 588636160 | bytes 6587648 | tf_op jit(solution)/shard_map/fc,rf->cr/dot_general | solution.py:56
  109.4 4.4 %copy.42 = bf16[3584,320]{1,0:T(8,128)(2,1)} copy(bf16[3584,320]{0,1:T(8,128)(2,1)} %fusion) | data formatting | bytes 4587520
  113.8 0.6 copy-done.4
  114.6 0.1 reshape.285
  114.9 44.6 %all-reduce = (f32[128,64]{0,1:T(8,128)S(1)}, f32[128]{0:T(128)S(1)}) all-reduce(f32[128,64]{0,1:T(8,128)S(1)} %fusion.24, f32[128]{0:T(128)S(1)} %multiply_reduce_fusion.2), channel_id=1, replica_groups=mesh['pipe'=16,'expert'=64] {'pipe'}, use_global_device_ids=true, to_apply=%region_2.0 | all-reduce | flops 8320 | bytes 66560 | tf_op jit(solution)/shard_map/psum | solution.py:19
  159.5 2.0 gather_fusion.1
  161.7 16.2 %reduce-scatter.4.cloned.1.call-done = bf16[224,320]{1,0:T(8,128)(2,1)} async-done(((bf16[3584,320]{1,0:T(8,128)(2,1)}), bf16[224,320]{1,0:T(8,128)(2,1)}) %reduce-scatter.4.cloned.1.call-update) | async-done | bytes 143376
  177.9 1.0 copy.43
  179.0 0.8 reshape.266
  179.8 11.3 %all-to-all-start.1 = ((bf16[64,5,224]{2,1,0:T(8,128)(2,1)}), bf16[64,5,224]{2,1,0:T(8,128)(2,1)S(1)}, u32[]{:S(2)}, u32[]{:S(2)}) async-start(bf16[64,5,224]{2,1,0:T(8,128)(2,1)} %reshape.266), calls=%async_computation.1 | async-start | bytes 524288 | tf_op jit(solution)/shard_map/all_to_all | solution.py:67
  191.2 12.4 %all-to-all-done.1 = bf16[64,5,224]{2,1,0:T(8,128)(2,1)S(1)} async-done(((bf16[64,5,224]{2,1,0:T(8,128)(2,1)}), bf16[64,5,224]{2,1,0:T(8,128)(2,1)S(1)}, u32[]{:S(2)}, u32[]{:S(2)}) %all-to-all-start.1) | async-done | bytes 143392 | tf_op jit(solution)/shard_map/all_to_all | solution.py:67
  203.7 1.2 gather_fusion
  204.9 0.1 reshape.268
  205.1 0.4 multiply_reduce_fusion.1
  205.5 0.7 copy.41
  (38 shorter events, 1.2 us)
Async XLA Ops:
  6.5 97.7 %copy-start = (bf16[1,128,3584]{2,1,0:T(8,128)(2,1)S(1)}, bf16[1,128,3584]{2,1,0:T(8,128)(2,1)}, u32[]{:S(2)}) copy-start(bf16[1,128,3584]{2,1,0:T(8,128)(2,1)} %param.11) | copy-start | bytes 2752516
  6.5 85.8 %all-gather.3.cloned.1.call-start = ((), (), s32[]{:S(2)}) async-start(), calls=%async_computation.3 | async-start | bytes 2785280 | tf_op jit(solution)/shard_map/all_gather | solution.py:45
  50.9 127.0 %reduce-scatter.4.cloned.1.call-start = ((), (), s32[]{:S(2)}) async-start(), calls=%async_computation.4 | async-start | bytes 2924544
  102.3 1.2 copy-start.1
  113.8 0.7 copy-start.4
  113.8 0.9 copy-start.2
  113.8 1.0 copy-start.3
  179.8 23.9 %all-to-all-start.1 = ((bf16[64,5,224]{2,1,0:T(8,128)(2,1)}), bf16[64,5,224]{2,1,0:T(8,128)(2,1)S(1)}, u32[]{:S(2)}, u32[]{:S(2)}) async-start(bf16[64,5,224]{2,1,0:T(8,128)(2,1)} %reshape.266), calls=%async_computation.1 | async-start | bytes 524288 | tf_op jit(solution)/shard_map/all_to_all | solution.py:67
Sparse Core Ops, SparseCore 0:
  51.0 41.2 all-gather.2
  113.9 63.9 reduce-scatter.3
where the time goes:
time: 217 us; the launch traced here: 213 us
  blocking collectives  80.2 us (37%)
  waiting for transfers between devices  70.1 us (32%)
  local copies, waits for them, and re-layouts  29.9 us (14%)
  between operations  13.6 us (6%)
  starting transfers between devices  11.3 us (5%)
  matrix products  6.04 us (3%)
    psum x1, blocking collectives, body(): square_sum, logits = lax.psum((part_square, part_logits), 'pipe')  44.6 us
    all_gather x1, waiting for transfers between devices, body(): piece = lax.all_gather(rows, 'pipe', axis=1, tiled=True)  41.4 us
    all_to_all x1, blocking collectives, body(): lax.all_to_all(outgoing.reshape(experts, capacity, part_width), 'expert',...  35.6 us
    unnamed x3, waiting for transfers between devices  16.2 us
    unnamed x16, local copies, waits for them, and re-layouts  13.7 us
    all_to_all x1, waiting for transfers between devices, body(): lax.all_to_all(expert_out, 'expert', split_axis=0, concat_axis=0, tiled=T...  12.4 us
    all_to_all x1, starting transfers between devices, body(): lax.all_to_all(expert_out, 'expert', split_axis=0, concat_axis=0, tiled=T...  11.3 us
    dot_general x1, matrix products, body(): jnp.einsum('fc,rf->cr', down_weight, hidden, preferred_element_type=jnp.f...  5.14 us
  transfers between devices with their start and end apart: 3, of which 3 were waited for; matrix products, arithmetic and copies ran while one was open for 1% of the time, Pallas kernels for 0%

commit v1 on v0

v1 whole, which is shorter than its diff:
```python
import functools

import jax
import jax.numpy as jnp
from jax import lax
from jax.experimental import pallas as pl
from jax.experimental.pallas import tpu as pltpu
from jax.sharding import PartitionSpec as P

eps = 1e-06
MESH = pl.DeviceIdType.MESH
BF = jnp.bfloat16
F32 = jnp.float32
SLOT = 8


def dot(a, b, ca=1, cb=0):
    return lax.dot_general(a, b, (((ca,), (cb,)), ((), ())), preferred_element_type=F32)


def iota(shape, axis):
    return lax.broadcasted_iota(jnp.int32, shape, axis)


def kernel(
    cfg,
    tok_hbm,
    routes_hbm,
    router_hbm,
    wg_hbm,
    wu_hbm,
    wd_hbm,
    out_ref,
    tokx,
    routes,
    router,
    wgx,
    wd_raw,
    wd_stage,
    wd_pair,
    place,
    outgoing,
    incoming,
    xg,
    acc,
    acc_ss,
    hid2,
    hid_own,
    rst,
    rsr,
    ret_out,
    ret_in,
    lg_send,
    lg_recv,
    load_sem,
    wload_sem,
    disp_send,
    disp_recv,
    disp_own,
    lg_ssem,
    lg_rsem,
    wd_sem,
    ag_ssem,
    ag_rsem,
    sib_ssem,
    sib_rsem,
    hid_ssem,
    hid_rsem,
    rs_ssem,
    rs_rsem,
    ret_send,
    ret_recv,
    ret_own,
):
    n_pipe, n_exp, nx, tok, topk, cap, pw, width = cfg
    ny = n_pipe // 2
    far = ny // 2
    nz = n_exp // nx
    lanes = xg.shape[2]
    fb = wd_raw.shape[0]
    rows = n_exp * cap
    half = rows // 2
    slots = n_exp * SLOT
    hslots = slots // 2
    me_p = lax.axis_index("pipe")
    me_e = lax.axis_index("expert")
    y = me_p // 2
    c = me_p % 2
    ez = me_e // nx
    ex = me_e % nx

    def peer_of(i):
        return ((ez + i // nx) % nz) * nx + (ex + i % nx) % nx

    def pipe_dev(rel):
        return {"pipe": 2 * ((y + rel + ny) % ny) + c}

    sib = {"pipe": 2 * y + 1 - c}

    load_tok = pltpu.make_async_copy(tok_hbm, tokx.at[pl.ds(0, pw)], load_sem.at[0])
    load_routes = pltpu.make_async_copy(routes_hbm, routes, load_sem.at[1])
    load_router = pltpu.make_async_copy(router_hbm, router, load_sem.at[2])
    load_wd = pltpu.make_async_copy(wd_hbm.at[0], wd_raw, load_sem.at[3])
    load_tok.start()
    load_routes.start()
    load_router.start()
    load_wd.start()

    barrier = pltpu.get_barrier_semaphore()

    def greet_expert(i, _):
        pl.semaphore_signal(barrier, inc=1, device_id={"expert": peer_of(i)}, device_id_type=MESH)
        return 0

    def greet_pipe(i, _):
        pl.semaphore_signal(
            barrier, inc=1, device_id={"pipe": (me_p + i) % n_pipe}, device_id_type=MESH
        )
        return 0

    lax.fori_loop(1, n_exp, greet_expert, 0)
    lax.fori_loop(1, n_pipe, greet_pipe, 0)

    def load_w(p, _):
        src = pl.ds(pl.multiple_of(p * pw, 16), pw)
        pltpu.make_async_copy(
            wg_hbm.at[0, src], wgx.at[p, pl.ds(0, pw), pl.ds(0, fb)], wload_sem.at[0]
        ).start()
        pltpu.make_async_copy(
            wu_hbm.at[0, src], wgx.at[p, pl.ds(0, pw), pl.ds(fb, fb)], wload_sem.at[1]
        ).start()
        return 0

    lax.fori_loop(0, n_pipe, load_w, 0)

    load_routes.wait()
    expert_of = iota((slots, tok), 0) // SLOT
    slot_of = (iota((slots, tok), 0) % SLOT).astype(F32)
    named = jnp.where(routes[0:1, :] == expert_of, 1.0, 0.0)
    for k in range(1, topk):
        named = named + jnp.where(routes[k : k + 1, :] == expert_of, 1.0, 0.0)
    earlier = jnp.where(iota((tok, tok), 0) < iota((tok, tok), 1), 1.0, 0.0).astype(BF)
    count = dot(named.astype(BF), earlier)
    placed = jnp.where(count == slot_of, named, 0.0)
    place[...] = placed

    load_tok.wait()
    tf = tokx[0:pw, :].astype(F32)
    square = jnp.sum(tf * tf, axis=0, keepdims=True)
    hi = square.astype(BF).astype(F32)
    mid = (square - hi).astype(BF).astype(F32)
    lo = square - hi - mid
    spare = iota((lanes - pw, tok), 0)
    tokx[pw:lanes, :] = jnp.where(
        spare == 0, hi, jnp.where(spare == 1, mid, jnp.where(spare == 2, lo, 0.0))
    ).astype(BF)
    outgoing[...] = (
        dot(placed.astype(BF), tokx[...], 1, 1).astype(BF).reshape(n_exp, SLOT, lanes)
    )

    pl.semaphore_wait(barrier, n_exp - 1 + n_pipe - 1)

    def dispatch(i, _):
        dest = peer_of(i)
        pltpu.make_async_remote_copy(
            src_ref=outgoing.at[dest],
            dst_ref=incoming.at[me_e],
            send_sem=disp_send,
            recv_sem=disp_recv,
            device_id={"expert": dest},
            device_id_type=MESH,
        ).start()
        return 0

    lax.fori_loop(1, n_exp, dispatch, 0)
    own_block = pltpu.make_async_copy(outgoing.at[me_e], incoming.at[me_e], disp_own)
    own_block.start()

    load_router.wait()
    part = dot(router[...], tokx[0:pw, :])
    picks = []
    for k in range(topk):
        picks.append(
            jnp.sum(
                jnp.where(iota((n_exp, tok), 0) == routes[k : k + 1, :], part, 0.0),
                axis=0,
                keepdims=True,
            )
        )
    row8 = iota((8, tok), 0)
    packed = jnp.where(row8 == topk, square, 0.0)
    for k in range(topk):
        packed = jnp.where(row8 == k, picks[k], packed)
    lg_send[...] = packed
    lg_recv[pl.ds(me_p, 1)] = packed[None]

    def send_logits(i, _):
        pltpu.make_async_remote_copy(
            src_ref=lg_send,
            dst_ref=lg_recv.at[me_p],
            send_sem=lg_ssem,
            recv_sem=lg_rsem,
            device_id={"pipe": (me_p + i) % n_pipe},
            device_id_type=MESH,
        ).start()
        return 0

    lax.fori_loop(1, n_pipe, send_logits, 0)

    load_wd.wait()
    for p in range(n_pipe):
        base = (pw * p) // 128 * 128
        off = pw * p - base
        span = min(-(-(off + pw) // 128) * 128, wd_raw.shape[1] - base)
        shift = (iota((span, lanes), 0) == iota((span, lanes), 1) + off) & (
            iota((span, lanes), 1) < pw
        )
        wd_stage[p % 2, p // 2] = dot(
            wd_raw[:, base : base + span], jnp.where(shift, 1.0, 0.0).astype(BF)
        ).astype(BF)
    wd_own = pltpu.make_async_copy(wd_stage.at[c], wd_pair.at[:, pl.ds(0, fb)], wd_sem.at[0])
    wd_own.start()
    wd_sib = pltpu.make_async_remote_copy(
        src_ref=wd_stage.at[1 - c],
        dst_ref=wd_pair.at[:, pl.ds(fb, fb)],
        send_sem=wd_sem.at[1],
        recv_sem=wd_sem.at[2],
        device_id=sib,
        device_id_type=MESH,
    )
    wd_sib.start()
    wgx[:, pw:lanes, :] = jnp.zeros((n_pipe, lanes - pw, 2 * fb), BF)
    for j in range(2):
        everything = wgx.at[:, pl.ds(0, pw), pl.ds(j * fb, fb)]
        pltpu.make_async_copy(everything, everything, wload_sem.at[j]).wait()

    slot_id = iota((half, hslots), 1)
    target = (slot_id // SLOT) * cap + slot_id % SLOT
    pick = jnp.where(
        (iota((half, hslots), 0) == target) & (slot_id % SLOT < cap), 1.0, 0.0
    ).astype(BF)
    own_block.wait()
    arrived = incoming.at[pl.ds(0, n_exp - 1)]
    pltpu.make_async_copy(arrived, arrived, disp_recv).wait()

    def block_of(rel):
        return 2 * ((y + rel + ny) % ny) + c

    def block_sib(rel):
        return 2 * ((y + rel + ny) % ny) + 1 - c

    def part_of(p, h):
        return xg.at[p, pl.ds(h * half, half)]

    def forward(way, d, h):
        sign = 1 if way == 0 else -1
        p = block_of(-sign * d)
        return pltpu.make_async_remote_copy(
            src_ref=part_of(p, h),
            dst_ref=part_of(p, h),
            send_sem=ag_ssem.at[way, d, h],
            recv_sem=ag_rsem.at[way, d, h],
            device_id=pipe_dev(sign),
            device_id_type=MESH,
        )

    def arrival(way, d, h):
        sign = 1 if way == 0 else -1
        p = block_of(-sign * d)
        return pltpu.make_async_remote_copy(
            src_ref=part_of(p, h),
            dst_ref=part_of(p, h),
            send_sem=ag_ssem.at[way, d - 1, h],
            recv_sem=ag_rsem.at[way, d - 1, h],
            device_id=pipe_dev(sign),
            device_id_type=MESH,
        )

    def to_sibling(rel, h):
        p = block_of(rel)
        return pltpu.make_async_remote_copy(
            src_ref=part_of(p, h),
            dst_ref=part_of(p, h),
            send_sem=sib_ssem.at[rel % ny, h],
            recv_sem=sib_rsem.at[rel % ny, h],
            device_id=sib,
            device_id_type=MESH,
        )

    def from_sibling(rel, h):
        p = block_sib(rel)
        return pltpu.make_async_remote_copy(
            src_ref=part_of(p, h),
            dst_ref=part_of(p, h),
            send_sem=sib_ssem.at[rel % ny, h],
            recv_sem=sib_rsem.at[rel % ny, h],
            device_id=sib,
            device_id_type=MESH,
        )

    def travels(way, d, h):
        return d < far - 1 or (d == far - 1 and h == way)

    sent = []

    def go(copy):
        copy.start()
        sent.append(copy)

    def gather_math(blocks, first=False):
        total = None
        total_ss = None
        for p in blocks:
            one = dot(xg[p], wgx[p])
            ss = xg[p, :, lanes - 128 : lanes].astype(F32)
            total = one if total is None else total + one
            total_ss = ss if total_ss is None else total_ss + ss
        if first:
            acc[...] = total
            acc_ss[...] = total_ss
        else:
            acc[...] += total
            acc_ss[...] += total_ss

    me_block = block_of(0)
    for h in range(2):
        flat = incoming[h * (n_exp // 2) : (h + 1) * (n_exp // 2)].reshape(hslots, lanes)
        xg[me_block, h * half : (h + 1) * half, :] = dot(pick, flat).astype(BF)
        for way in range(2):
            if travels(way, 0, h):
                go(forward(way, 0, h))
        go(to_sibling(0, h))
    gather_math([me_block], first=True)
    for d in range(1, far):
        for h in range(2):
            for way in range(2):
                rel = -d if way == 0 else d
                arrival(way, d, h).wait_recv()
                if travels(way, d, h):
                    go(forward(way, d, h))
                go(to_sibling(rel, h))
        behind = [0] if d == 1 else [-(d - 1), d - 1]
        for rel in behind:
            for h in range(2):
                from_sibling(rel, h).wait_recv()
        gather_math(
            [block_sib(rel) for rel in behind] + [block_of(-d), block_of(d)]
        )
    for h in range(2):
        arrival(h, far, h).wait_recv()
        go(to_sibling(far, h))
    behind = [-(far - 1), far - 1] if far > 1 else [0]
    for rel in behind:
        for h in range(2):
            from_sibling(rel, h).wait_recv()
    gather_math([block_sib(rel) for rel in behind] + [block_of(far)])
    for h in range(2):
        from_sibling(far, h).wait_recv()
    gather_math([block_sib(far)])

    first_spare = pw - (lanes - 128)
    hid_copies = []
    for h in range(2):
        r = slice(h * half, (h + 1) * half)
        ss_lane = iota((half, 128), 1)
        ss = jnp.where((ss_lane >= first_spare) & (ss_lane < first_spare + 3), acc_ss[r, :], 0.0)
        scale = lax.rsqrt(jnp.sum(ss, axis=1, keepdims=True) / width + eps)
        gate = scale * acc[r, 0:fb]
        up = scale * acc[r, fb : 2 * fb]
        hidden = ((gate / (1.0 + jnp.exp(-gate))) * up).astype(BF)
        hid2[r, 0:fb] = hidden
        hid_own[r, :] = hidden
        copy = pltpu.make_async_remote_copy(
            src_ref=hid_own.at[pl.ds(h * half, half)],
            dst_ref=hid2.at[pl.ds(h * half, half), pl.ds(fb, fb)],
            send_sem=hid_ssem.at[h],
            recv_sem=hid_rsem.at[h],
            device_id=sib,
            device_id_type=MESH,
        )
        copy.start()
        hid_copies.append(copy)
    wd_own.wait()
    wd_sib.wait()
    for copy in hid_copies:
        copy.wait()

    def contribution(rel, h):
        return dot(hid2[h * half : (h + 1) * half, :], wd_pair[(y + rel + ny) % ny])

    def pass_on(way, s, h):
        sign = 1 if way == 0 else -1
        return pltpu.make_async_remote_copy(
            src_ref=rst.at[way, s, h],
            dst_ref=rsr.at[way, s, h],
            send_sem=rs_ssem.at[way, s, h],
            recv_sem=rs_rsem.at[way, s, h],
            device_id=pipe_dev(sign),
            device_id_type=MESH,
        )

    for s in range(far):
        for turn in range(2):
            for way in range(2):
                h = 1 - way if turn == 0 else way
                if s == 0 and h != way:
                    continue
                rel = (far - s) * (1 if way == 0 else -1)
                total = contribution(rel, h)
                if s > 1 or (s == 1 and h == way):
                    pass_on(way, s - 1, h).wait_recv()
                    total = total + rsr[way, s - 1, h].astype(F32)
                rst[way, s, h] = total.astype(BF)
                go(pass_on(way, s, h))

    spread = (iota((hslots, half), 0) // SLOT) * cap + iota((hslots, half), 0) % SLOT
    unpick = jnp.where(
        (iota((hslots, half), 1) == spread) & (iota((hslots, half), 0) % SLOT < cap), 1.0, 0.0
    ).astype(BF)
    for h in range(2):
        total = contribution(0, h)
        for way in range(2):
            if far > 1 or h == way:
                pass_on(way, far - 1, h).wait_recv()
                total = total + rsr[way, far - 1, h].astype(F32)
        ret_out[h * (n_exp // 2) : (h + 1) * (n_exp // 2)] = (
            dot(unpick, total.astype(BF)).astype(BF).reshape(n_exp // 2, SLOT, lanes)
        )

    def give_back(i, _):
        dest = peer_of(i)
        pltpu.make_async_remote_copy(
            src_ref=ret_out.at[dest],
            dst_ref=ret_in.at[me_e],
            send_sem=ret_send,
            recv_sem=ret_recv,
            device_id={"expert": dest},
            device_id_type=MESH,
        ).start()
        return 0

    lax.fori_loop(1, n_exp, give_back, 0)
    own_back = pltpu.make_async_copy(ret_out.at[me_e], ret_in.at[me_e], ret_own)
    own_back.start()

    others = lg_recv.at[pl.ds(0, n_pipe - 1)]
    pltpu.make_async_copy(others, others, lg_rsem).wait()
    sums = jnp.sum(lg_recv[...], axis=0)
    rstd = lax.rsqrt(sums[topk : topk + 1, :] / width + eps)
    scores = []
    for k in range(topk):
        logit = rstd * sums[k : k + 1, :]
        small = jnp.exp(-jnp.abs(logit))
        scores.append(jnp.where(logit >= 0, 1.0, small) / (1.0 + small))
    norm = scores[0]
    for k in range(1, topk):
        norm = norm + scores[k]
    weighted = jnp.zeros((slots, tok), F32)
    for k in range(topk):
        weighted = jnp.where(routes[k : k + 1, :] == expert_of, scores[k] / norm, weighted)
    weighted = weighted * place[...]
    w_hi = weighted.astype(BF)
    w_lo = (weighted - w_hi.astype(F32)).astype(BF)

    for copy in sent:
        copy.wait_send()
    block63 = outgoing.at[pl.ds(0, n_exp - 1)]
    pltpu.make_async_copy(block63, block63, disp_send).wait()
    sent15 = lg_recv.at[pl.ds(0, n_pipe - 1)]
    pltpu.make_async_copy(sent15, sent15, lg_ssem).wait()

    own_back.wait()
    back63 = ret_in.at[pl.ds(0, n_exp - 1)]
    pltpu.make_async_copy(back63, back63, ret_recv).wait()
    got = ret_in[...].reshape(slots, lanes)
    mixed = dot(got, w_hi, 0, 0) + dot(got, w_lo, 0, 0)
    out_ref[...] = mixed[0:pw, :].astype(BF)
    left63 = ret_out.at[pl.ds(0, n_exp - 1)]
    pltpu.make_async_copy(left63, left63, ret_send).wait()


def body(tokens, routes, router, w_gate, w_up, w_down):
    tok, pw = tokens.shape
    topk = routes.shape[1]
    n_exp = lax.axis_size("expert")
    n_pipe = lax.axis_size("pipe")
    cap = max(2, tok * topk // n_exp + max(1, tok * topk // (4 * n_exp)))
    width = pw * n_pipe
    lanes = -(-(pw + 3) // 128) * 128
    fb = w_gate.shape[2]
    ny = n_pipe // 2
    far = ny // 2
    rows = n_exp * cap
    half = rows // 2
    nx = 8 if n_exp % 8 == 0 else n_exp
    cfg = (n_pipe, n_exp, nx, tok, topk, cap, pw, width)
    dma = pltpu.SemaphoreType.DMA
    scratch = [
        pltpu.VMEM((lanes, tok), BF),
        pltpu.VMEM((topk, tok), jnp.int32),
        pltpu.VMEM((n_exp, pw), BF),
        pltpu.VMEM((n_pipe, lanes, 2 * fb), BF),
        pltpu.VMEM((fb, width), BF),
        pltpu.VMEM((2, ny, fb, lanes), BF),
        pltpu.VMEM((ny, 2 * fb, lanes), BF),
        pltpu.VMEM((n_exp * SLOT, tok), F32),
        pltpu.VMEM((n_exp, SLOT, lanes), BF),
        pltpu.VMEM((n_exp, SLOT, lanes), BF),
        pltpu.VMEM((n_pipe, rows, lanes), BF),
        pltpu.VMEM((rows, 2 * fb), F32),
        pltpu.VMEM((rows, 128), F32),
        pltpu.VMEM((rows, 2 * fb), BF),
        pltpu.VMEM((rows, fb), BF),
        pltpu.VMEM((2, far, 2, half, lanes), BF),
        pltpu.VMEM((2, far, 2, half, lanes), BF),
        pltpu.VMEM((n_exp, SLOT, lanes), BF),
        pltpu.VMEM((n_exp, SLOT, lanes), BF),
        pltpu.VMEM((8, tok), F32),
        pltpu.VMEM((n_pipe, 8, tok), F32),
        dma((4,)),
        dma((2,)),
        dma,
        dma,
        dma,
        dma,
        dma,
        dma((3,)),
        dma((2, far, 2)),
        dma((2, far, 2)),
        dma((ny, 2)),
        dma((ny, 2)),
        dma((2,)),
        dma((2,)),
        dma((2, far, 2)),
        dma((2, far, 2)),
        dma,
        dma,
        dma,
    ]
    mixed = pl.pallas_call(
        functools.partial(kernel, cfg),
        out_shape=jax.ShapeDtypeStruct((pw, tok), BF),
        in_specs=[pl.BlockSpec(memory_space=pl.ANY)] * 6,
        out_specs=pl.BlockSpec(memory_space=pltpu.VMEM),
        scratch_shapes=scratch,
        compiler_params=pltpu.CompilerParams(
            collective_id=0, has_side_effects=True, vmem_limit_bytes=40 << 20
        ),
    )(tokens.T, routes.T, router.T, w_gate, w_up, w_down)
    return mixed.T


def solution(mesh):
    placed = (
        P("expert", "pipe"),
        P("expert", None),
        P("pipe", None),
        P("expert", None, "pipe"),
        P("expert", None, "pipe"),
        P("expert", "pipe", None),
    )
    return jax.shard_map(
        body, mesh=mesh, in_specs=placed, out_specs=P("expert", "pipe"), check_vma=False
    )
```

time: 217 us -> 90.4 us (0.42); the launches traced: 213 us -> 90 us
  Pallas kernels: 0 us -> 83.6 us
  blocking collectives: 80.2 us -> 0 us
  waiting for transfers between devices: 70.1 us -> 0 us
  local copies, waits for them, and re-layouts: 29.9 us -> 6.41 us
  between operations: 13.6 us -> 0.02 us
  starting transfers between devices: 11.3 us -> 0 us
  matrix products: 6.04 us -> 0 us
    pallas_call x0 -> x1, Pallas kernels: none -> 83.6 us  [body(): pl.pallas_call(functools.partial(kernel, cfg), out_shape=jax.ShapeDtypeSt...]
    psum x1 -> x0, blocking collectives: 44.6 us -> none  [body(): square_sum, logits = lax.psum((part_square, part_logits), 'pipe')]
    all_gather x1 -> x0, waiting for transfers between devices: 41.4 us -> none  [body(): piece = lax.all_gather(rows, 'pipe', axis=1, tiled=True)]
    all_to_all x1 -> x0, blocking collectives: 35.6 us -> none  [body(): lax.all_to_all(outgoing.reshape(experts, capacity, part_width), 'expert',...]
    unnamed x3 -> x0, waiting for transfers between devices: 16.2 us -> none
    all_to_all x1 -> x0, waiting for transfers between devices: 12.4 us -> none  [body(): lax.all_to_all(expert_out, 'expert', split_axis=0, concat_axis=0, tiled=T...]
    all_to_all x1 -> x0, starting transfers between devices: 11.3 us -> none  [body(): lax.all_to_all(expert_out, 'expert', split_axis=0, concat_axis=0, tiled=T...]
    unnamed x16 -> x13, local copies, waits for them, and re-layouts: 13.7 us -> 6.41 us
  transfers between devices with their start and end apart: 3 -> 0, of which waited for: 3 -> 0; matrix products, arithmetic and copies ran while one was open for 1% -> 0% of each run, Pallas kernels for 0% -> 0%
where the time goes in v1:
time: 90.4 us; the launch traced here: 90 us
  Pallas kernels  83.6 us (92%)
  local copies, waits for them, and re-layouts  6.41 us (7%)
    pallas_call x1, Pallas kernels, body(): pl.pallas_call(functools.partial(kernel, cfg), out_shape=jax.ShapeDtypeSt...  83.6 us
    unnamed x13, local copies, waits for them, and re-layouts  6.41 us

profile of v1, /device:TPU:1, one launch (start us, length us, event | category | flops | bytes accessed | tf_op | source)
XLA Modules:
  0.0 90.0 jit_solution(37085243986528979)
XLA Ops:
  0.0 0.0 copy-start.5
  0.0 0.7 copy-done.5
  0.7 0.0 copy-start
  0.7 1.2 %copy-done = bf16[1,3584,128]{2,1,0:T(8,128)(2,1)S(1)} copy-done((bf16[1,3584,128]{2,1,0:T(8,128)(2,1)S(1)}, bf16[1,3584,128]{2,1,0:T(8,128)(2,1)}, u32[]{:S(2)}) %copy-start) | copy-done | bytes 917528
  1.9 0.0 copy-start.1
  1.9 1.2 %copy-done.1 = bf16[1,3584,128]{2,1,0:T(8,128)(2,1)S(1)} copy-done((bf16[1,3584,128]{2,1,0:T(8,128)(2,1)S(1)}, bf16[1,3584,128]{2,1,0:T(8,128)(2,1)}, u32[]{:S(2)}) %copy-start.1) | copy-done | bytes 917528
  3.0 0.0 copy-start.2
  3.0 1.2 %copy-done.2 = bf16[1,128,3584]{2,1,0:T(8,128)(2,1)S(1)} copy-done((bf16[1,128,3584]{2,1,0:T(8,128)(2,1)S(1)}, bf16[1,128,3584]{2,1,0:T(8,128)(2,1)}, u32[]{:S(2)}) %copy-start.2) | copy-done | bytes 917528
  4.2 0.0 copy-start.3
  4.2 0.8 copy-done.3
  5.0 0.0 copy-start.4
  5.0 0.8 copy-done.4
  5.8 83.6 %shard_map.64 = bf16[224,128]{1,0:T(8,128)(2,1)S(1)} custom-call(bf16[224,128]{1,0:T(8,128)(2,1)S(1)} %bitcast.5, s32[2,128]{1,0:T(2,128)S(1)} %bitcast.7, bf16[64,224]{1,0:T(8,128)(2,1)S(1)} %bitcast.6, bf16[1,3584,128]{2,1,0:T(8,128)(2,1)S(1)} %copy-done, bf16[1,3584,128]{2,1,0:T(8,128)(2,1)S(1)} %copy-done.1, bf16[1,128,3584]{2,1,0:T(8,128)(2,1)S(1)} %copy-done.2), custom_call_target="tpu_custom_call" | custom-call | tf_op jit(solution)/shard_map/pallas_call | solution.py:540
  89.4 0.6 copy.8
Async XLA Ops:
  0.0 0.7 copy-start.5
  0.7 1.2 %copy-start = (bf16[1,3584,128]{2,1,0:T(8,128)(2,1)S(1)}, bf16[1,3584,128]{2,1,0:T(8,128)(2,1)}, u32[]{:S(2)}) copy-start(bf16[1,3584,128]{2,1,0:T(8,128)(2,1)} %wg_hbm.1) | copy-start | bytes 2752516
  1.9 1.2 %copy-start.1 = (bf16[1,3584,128]{2,1,0:T(8,128)(2,1)S(1)}, bf16[1,3584,128]{2,1,0:T(8,128)(2,1)}, u32[]{:S(2)}) copy-start(bf16[1,3584,128]{2,1,0:T(8,128)(2,1)} %wu_hbm.1) | copy-start | bytes 2752516
  3.0 1.2 %copy-start.2 = (bf16[1,128,3584]{2,1,0:T(8,128)(2,1)S(1)}, bf16[1,128,3584]{2,1,0:T(8,128)(2,1)}, u32[]{:S(2)}) copy-start(bf16[1,128,3584]{2,1,0:T(8,128)(2,1)} %wd_hbm.1) | copy-start | bytes 2752516
  4.2 0.8 copy-start.3
  5.0 0.8 copy-start.4

commit v2 on v1

--- a/solution.py
+++ b/solution.py
@@ -72,16 +72,17 @@
     ret_recv,
     ret_own,
 ):
-    n_pipe, n_exp, nx, tok, topk, cap, pw, width = cfg
+    n_pipe, n_exp, nx, tok, topk, cap, pw, width, turns = cfg
     ny = n_pipe // 2
     far = ny // 2
     nz = n_exp // nx
     lanes = xg.shape[2]
     fb = wd_raw.shape[0]
     rows = n_exp * cap
-    half = rows // 2
+    half = rows // turns
     slots = n_exp * SLOT
-    hslots = slots // 2
+    hslots = slots // turns
+    group = n_exp // turns
     me_p = lax.axis_index("pipe")
     me_e = lax.axis_index("expert")
     y = me_p // 2
@@ -89,8 +90,30 @@
     ez = me_e // nx
     ex = me_e % nx
 
+    def offset(i):
+        if nz < 4:
+            return 0, i % nx
+        row, col = nz - 1 - i // nx, i % nx
+        dz = jnp.where(row % 2 == 1, (row + 1) // 2, nz - (row + 1) // 2)
+        return dz, col + nx // 2
+
+    self_step = 0 if nz < 4 else (nz - 1) * nx + nx // 2
+    self_turn = self_step // group
+
     def peer_of(i):
-        return ((ez + i // nx) % nz) * nx + (ex + i % nx) % nx
+        dz, dx = offset(i)
+        return ((ez + dz) % nz) * nx + (ex + dx) % nx
+
+    def source_of(i):
+        dz, dx = offset(i)
+        return ((ez + 2 * nz - dz) % nz) * nx + (ex + 2 * nx - dx) % nx
+
+    def each_step(low, high, do):
+        if low <= self_step < high:
+            lax.fori_loop(low, self_step, do, 0)
+            lax.fori_loop(self_step + 1, high, do, 0)
+        else:
+            lax.fori_loop(low, high, do, 0)
 
     def pipe_dev(rel):
         return {"pipe": 2 * ((y + rel + ny) % ny) + c}
@@ -118,7 +141,7 @@
         )
         return 0
 
-    lax.fori_loop(1, n_exp, greet_expert, 0)
+    each_step(0, n_exp, greet_expert)
     lax.fori_loop(1, n_pipe, greet_pipe, 0)
 
     def load_w(p, _):
@@ -164,17 +187,17 @@
         dest = peer_of(i)
         pltpu.make_async_remote_copy(
             src_ref=outgoing.at[dest],
-            dst_ref=incoming.at[me_e],
+            dst_ref=incoming.at[i],
             send_sem=disp_send,
-            recv_sem=disp_recv,
+            recv_sem=disp_recv.at[i // group],
             device_id={"expert": dest},
             device_id_type=MESH,
         ).start()
         return 0
 
-    lax.fori_loop(1, n_exp, dispatch, 0)
-    own_block = pltpu.make_async_copy(outgoing.at[me_e], incoming.at[me_e], disp_own)
+    own_block = pltpu.make_async_copy(outgoing.at[me_e], incoming.at[self_step], disp_own)
     own_block.start()
+    each_step(0, n_exp, dispatch)
 
     load_router.wait()
     part = dot(router[...], tokx[0:pw, :])
@@ -239,9 +262,6 @@
     pick = jnp.where(
         (iota((half, hslots), 0) == target) & (slot_id % SLOT < cap), 1.0, 0.0
     ).astype(BF)
-    own_block.wait()
-    arrived = incoming.at[pl.ds(0, n_exp - 1)]
-    pltpu.make_async_copy(arrived, arrived, disp_recv).wait()
 
     def block_of(rel):
         return 2 * ((y + rel + ny) % ny) + c
@@ -299,7 +319,7 @@
         )
 
     def travels(way, d, h):
-        return d < far - 1 or (d == far - 1 and h == way)
+        return d < far - 1 or (d == far - 1 and h % 2 == way)
 
     sent = []
 
@@ -307,60 +327,63 @@
         copy.start()
         sent.append(copy)
 
-    def gather_math(blocks, first=False):
+    def gather_math(blocks, h, first=False):
+        r = slice(h * half, (h + 1) * half)
         total = None
         total_ss = None
         for p in blocks:
-            one = dot(xg[p], wgx[p])
-            ss = xg[p, :, lanes - 128 : lanes].astype(F32)
+            one = dot(xg[p, r, :], wgx[p])
+            ss = xg[p, r, lanes - 128 : lanes].astype(F32)
             total = one if total is None else total + one
             total_ss = ss if total_ss is None else total_ss + ss
         if first:
-            acc[...] = total
-            acc_ss[...] = total_ss
+            acc[r, :] = total
+            acc_ss[r, :] = total_ss
         else:
-            acc[...] += total
-            acc_ss[...] += total_ss
-
-    me_block = block_of(0)
-    for h in range(2):
-        flat = incoming[h * (n_exp // 2) : (h + 1) * (n_exp // 2)].reshape(hslots, lanes)
+            acc[r, :] += total
+            acc_ss[r, :] += total_ss
+
+    def start_gather(h):
+        here = group - 1 if h == self_turn else group
+        if h == self_turn:
+            own_block.wait()
+        if here > 0:
+            arrived = incoming.at[pl.ds(0, here)]
+            pltpu.make_async_copy(arrived, arrived, disp_recv.at[h]).wait()
+        flat = incoming[h * group : (h + 1) * group].reshape(hslots, lanes)
+        me_block = block_of(0)
         xg[me_block, h * half : (h + 1) * half, :] = dot(pick, flat).astype(BF)
         for way in range(2):
             if travels(way, 0, h):
                 go(forward(way, 0, h))
         go(to_sibling(0, h))
-    gather_math([me_block], first=True)
-    for d in range(1, far):
-        for h in range(2):
-            for way in range(2):
-                rel = -d if way == 0 else d
-                arrival(way, d, h).wait_recv()
-                if travels(way, d, h):
-                    go(forward(way, d, h))
-                go(to_sibling(rel, h))
+        gather_math([me_block], h, first=True)
+
+    def step_gather(d, h):
+        for way in range(2):
+            rel = -d if way == 0 else d
+            arrival(way, d, h).wait_recv()
+            if travels(way, d, h):
+                go(forward(way, d, h))
+            go(to_sibling(rel, h))
         behind = [0] if d == 1 else [-(d - 1), d - 1]
         for rel in behind:
-            for h in range(2):
-                from_sibling(rel, h).wait_recv()
-        gather_math(
-            [block_sib(rel) for rel in behind] + [block_of(-d), block_of(d)]
-        )
-    for h in range(2):
-        arrival(h, far, h).wait_recv()
+            from_sibling(rel, h).wait_recv()
+        gather_math([block_sib(rel) for rel in behind] + [block_of(-d), block_of(d)], h)
+
+    def end_gather(h):
+        arrival(h % 2, far, h).wait_recv()
         go(to_sibling(far, h))
-    behind = [-(far - 1), far - 1] if far > 1 else [0]
-    for rel in behind:
-        for h in range(2):
+        behind = [-(far - 1), far - 1] if far > 1 else [0]
+        for rel in behind:
             from_sibling(rel, h).wait_recv()
-    gather_math([block_sib(rel) for rel in behind] + [block_of(far)])
-    for h in range(2):
+        gather_math([block_sib(rel) for rel in behind] + [block_of(far)], h)
         from_sibling(far, h).wait_recv()
-    gather_math([block_sib(far)])
+        gather_math([block_sib(far)], h)
 
     first_spare = pw - (lanes - 128)
-    hid_copies = []
-    for h in range(2):
+
+    def share_hidden(h):
         r = slice(h * half, (h + 1) * half)
         ss_lane = iota((half, 128), 1)
         ss = jnp.where((ss_lane >= first_spare) & (ss_lane < first_spare + 3), acc_ss[r, :], 0.0)
@@ -378,12 +401,8 @@
             device_id=sib,
             device_id_type=MESH,
         )
-        copy.start()
-        hid_copies.append(copy)
-    wd_own.wait()
-    wd_sib.wait()
-    for copy in hid_copies:
-        copy.wait()
+        go(copy)
+        return copy
 
     def contribution(rel, h):
         return dot(hid2[h * half : (h + 1) * half, :], wd_pair[(y + rel + ny) % ny])
@@ -399,49 +418,76 @@
             device_id_type=MESH,
         )
 
-    for s in range(far):
-        for turn in range(2):
-            for way in range(2):
-                h = 1 - way if turn == 0 else way
-                if s == 0 and h != way:
-                    continue
-                rel = (far - s) * (1 if way == 0 else -1)
-                total = contribution(rel, h)
-                if s > 1 or (s == 1 and h == way):
-                    pass_on(way, s - 1, h).wait_recv()
-                    total = total + rsr[way, s - 1, h].astype(F32)
-                rst[way, s, h] = total.astype(BF)
-                go(pass_on(way, s, h))
+    def add_and_pass(way, s, h, adds):
+        total = contribution((far - s) * (1 if way == 0 else -1), h)
+        if adds:
+            pass_on(way, s - 1, h).wait_recv()
+            total = total + rsr[way, s - 1, h].astype(F32)
+        rst[way, s, h] = total.astype(BF)
+        go(pass_on(way, s, h))
+
+    def start_scatter(h):
+        add_and_pass(h % 2, 0, h, False)
+        if far > 1:
+            add_and_pass(1 - h % 2, 1, h, False)
+
+    def step_scatter(s, h):
+        add_and_pass(h % 2, s, h, True)
+        if s + 1 < far:
+            add_and_pass(1 - h % 2, s + 1, h, True)
 
     spread = (iota((hslots, half), 0) // SLOT) * cap + iota((hslots, half), 0) % SLOT
     unpick = jnp.where(
         (iota((hslots, half), 1) == spread) & (iota((hslots, half), 0) % SLOT < cap), 1.0, 0.0
     ).astype(BF)
-    for h in range(2):
-        total = contribution(0, h)
-        for way in range(2):
-            if far > 1 or h == way:
-                pass_on(way, far - 1, h).wait_recv()
-                total = total + rsr[way, far - 1, h].astype(F32)
-        ret_out[h * (n_exp // 2) : (h + 1) * (n_exp // 2)] = (
-            dot(unpick, total.astype(BF)).astype(BF).reshape(n_exp // 2, SLOT, lanes)
-        )
 
     def give_back(i, _):
-        dest = peer_of(i)
         pltpu.make_async_remote_copy(
-            src_ref=ret_out.at[dest],
+            src_ref=ret_out.at[i],
             dst_ref=ret_in.at[me_e],
             send_sem=ret_send,
             recv_sem=ret_recv,
-            device_id={"expert": dest},
+            device_id={"expert": source_of(i)},
             device_id_type=MESH,
         ).start()
         return 0
 
-    lax.fori_loop(1, n_exp, give_back, 0)
-    own_back = pltpu.make_async_copy(ret_out.at[me_e], ret_in.at[me_e], ret_own)
-    own_back.start()
+    own_back = pltpu.make_async_copy(ret_out.at[self_step], ret_in.at[me_e], ret_own)
+
+    def end_scatter(h):
+        total = contribution(0, h)
+        for way in range(2):
+            if far > 1 or h % 2 == way:
+                pass_on(way, far - 1, h).wait_recv()
+                total = total + rsr[way, far - 1, h].astype(F32)
+        ret_out[h * group : (h + 1) * group] = (
+            dot(unpick, total.astype(BF)).astype(BF).reshape(group, SLOT, lanes)
+        )
+        each_step(h * group, (h + 1) * group, give_back)
+        if h == self_turn:
+            own_back.start()
+
+    for h in range(turns):
+        start_gather(h)
+    for d in range(1, far):
+        for h in range(turns):
+            step_gather(d, h)
+    wd_own.wait()
+    wd_sib.wait()
+    end_gather(0)
+    hid_copy = share_hidden(0)
+    for h in range(turns):
+        if h + 1 < turns:
+            end_gather(h + 1)
+        hid_copy.wait_recv()
+        start_scatter(h)
+        if h + 1 < turns:
+            hid_copy = share_hidden(h + 1)
+    for t in range(1, far):
+        for h in range(turns):
+            step_scatter(t, h)
+    for h in range(turns):
+        end_scatter(h)
 
     others = lg_recv.at[pl.ds(0, n_pipe - 1)]
     pltpu.make_async_copy(others, others, lg_rsem).wait()
@@ -461,6 +507,7 @@
     weighted = weighted * place[...]
     w_hi = weighted.astype(BF)
     w_lo = (weighted - w_hi.astype(F32)).astype(BF)
+    w_both = jnp.concatenate([w_hi, w_lo], axis=1)
 
     for copy in sent:
         copy.wait_send()
@@ -473,8 +520,8 @@
     back63 = ret_in.at[pl.ds(0, n_exp - 1)]
     pltpu.make_async_copy(back63, back63, ret_recv).wait()
     got = ret_in[...].reshape(slots, lanes)
-    mixed = dot(got, w_hi, 0, 0) + dot(got, w_lo, 0, 0)
-    out_ref[...] = mixed[0:pw, :].astype(BF)
+    both = dot(got, w_both, 0, 0)
+    out_ref[...] = (both[0:pw, 0:tok] + both[0:pw, tok : 2 * tok]).astype(BF)
     left63 = ret_out.at[pl.ds(0, n_exp - 1)]
     pltpu.make_async_copy(left63, left63, ret_send).wait()
 
@@ -491,9 +538,9 @@
     ny = n_pipe // 2
     far = ny // 2
     rows = n_exp * cap
-    half = rows // 2
     nx = 8 if n_exp % 8 == 0 else n_exp
-    cfg = (n_pipe, n_exp, nx, tok, topk, cap, pw, width)
+    turns = 4 if n_exp % 4 == 0 else 2
+    cfg = (n_pipe, n_exp, nx, tok, topk, cap, pw, width, turns)
     dma = pltpu.SemaphoreType.DMA
     scratch = [
         pltpu.VMEM((lanes, tok), BF),
@@ -511,8 +558,8 @@
         pltpu.VMEM((rows, 128), F32),
         pltpu.VMEM((rows, 2 * fb), BF),
         pltpu.VMEM((rows, fb), BF),
-        pltpu.VMEM((2, far, 2, half, lanes), BF),
-        pltpu.VMEM((2, far, 2, half, lanes), BF),
+        pltpu.VMEM((2, far, turns, rows // turns, lanes), BF),
+        pltpu.VMEM((2, far, turns, rows // turns, lanes), BF),
         pltpu.VMEM((n_exp, SLOT, lanes), BF),
         pltpu.VMEM((n_exp, SLOT, lanes), BF),
         pltpu.VMEM((8, tok), F32),
@@ -520,19 +567,19 @@
         dma((4,)),
         dma((2,)),
         dma,
-        dma,
+        dma((turns,)),
         dma,
         dma,
         dma,
         dma((3,)),
-        dma((2, far, 2)),
-        dma((2, far, 2)),
-        dma((ny, 2)),
-        dma((ny, 2)),
-        dma((2,)),
-        dma((2,)),
-        dma((2, far, 2)),
-        dma((2, far, 2)),
+        dma((2, far, turns)),
+        dma((2, far, turns)),
+        dma((ny, turns)),
+        dma((ny, turns)),
+        dma((turns,)),
+        dma((turns,)),
+        dma((2, far, turns)),
+        dma((2, far, turns)),
         dma,
         dma,
         dma,
@@ -544,7 +591,7 @@
         out_specs=pl.BlockSpec(memory_space=pltpu.VMEM),
         scratch_shapes=scratch,
         compiler_params=pltpu.CompilerParams(
-            collective_id=0, has_side_effects=True, vmem_limit_bytes=40 << 20
+            collective_id=0, has_side_effects=True, vmem_limit_bytes=60 << 20
         ),
     )(tokens.T, routes.T, router.T, w_gate, w_up, w_down)
     return mixed.T

time: 90.4 us -> 80.3 us (0.89)
  Pallas kernels: 83.6 us -> 78.6 us
  local copies, waits for them, and re-layouts: 6.41 us -> 1.45 us
    unnamed x13 -> x1, local copies, waits for them, and re-layouts: 6.41 us -> 1.45 us
    pallas_call x1, Pallas kernels: 83.6 us -> 78.6 us  [body(): pl.pallas_call(functools.partial(kernel, cfg), out_shape=jax.ShapeDtypeSt...]
where the time goes in v2:
time: 80.3 us; the launch traced here: 80.1 us
  Pallas kernels  78.6 us (98%)
  local copies, waits for them, and re-layouts  1.45 us (2%)
    pallas_call x1, Pallas kernels, body(): pl.pallas_call(functools.partial(kernel, cfg), out_shape=jax.ShapeDtypeSt...  78.6 us

profile of v2, /device:TPU:1, one launch (start us, length us, event | category | flops | bytes accessed | tf_op | source)
XLA Modules:
  0.0 80.1 jit_solution(1733016969358340612)
XLA Ops:
  0.0 78.6 %shard_map.64 = bf16[224,128]{1,0:T(8,128)(2,1)} custom-call(bf16[224,128]{1,0:T(8,128)(2,1)} %bitcast.5, s32[2,128]{1,0:T(2,128)} %bitcast.7, bf16[64,224]{1,0:T(8,128)(2,1)} %bitcast.6, bf16[1,3584,128]{2,1,0:T(8,128)(2,1)} %wg_hbm.1, bf16[1,3584,128]{2,1,0:T(8,128)(2,1)} %wu_hbm.1, bf16[1,128,3584]{2,1,0:T(8,128)(2,1)} %wd_hbm.1), custom_call_target="tpu_custom_call" | custom-call | tf_op jit(solution)/shard_map/pallas_call | solution.py:587
  78.7 1.4 %copy.8 = bf16[128,224]{0,1:T(8,128)(2,1)} copy(bf16[128,224]{0,1:T(8,128)(2,1)} %bitcast.4) | data formatting | bytes 114688

commit v3 on v2

--- a/solution.py
+++ b/solution.py
@@ -327,8 +327,8 @@
         copy.start()
         sent.append(copy)
 
-    def gather_math(blocks, h, first=False):
-        r = slice(h * half, (h + 1) * half)
+    def gather_math(blocks, h=None, first=False):
+        r = slice(0, rows) if h is None else slice(h * half, (h + 1) * half)
         total = None
         total_ss = None
         for p in blocks:
@@ -357,7 +357,6 @@
             if travels(way, 0, h):
                 go(forward(way, 0, h))
         go(to_sibling(0, h))
-        gather_math([me_block], h, first=True)
 
     def step_gather(d, h):
         for way in range(2):
@@ -366,18 +365,20 @@
             if travels(way, d, h):
                 go(forward(way, d, h))
             go(to_sibling(rel, h))
-        behind = [0] if d == 1 else [-(d - 1), d - 1]
+
+    def sibling_math(d):
+        behind = [0] if d == 0 else [-d, d]
         for rel in behind:
-            from_sibling(rel, h).wait_recv()
-        gather_math([block_sib(rel) for rel in behind] + [block_of(-d), block_of(d)], h)
-
-    def end_gather(h):
+            for h in range(turns):
+                from_sibling(rel, h).wait_recv()
+        gather_math([block_sib(rel) for rel in behind])
+
+    def last_block(h):
         arrival(h % 2, far, h).wait_recv()
         go(to_sibling(far, h))
-        behind = [-(far - 1), far - 1] if far > 1 else [0]
-        for rel in behind:
-            from_sibling(rel, h).wait_recv()
-        gather_math([block_sib(rel) for rel in behind] + [block_of(far)], h)
+        gather_math([block_of(far)], h)
+
+    def last_sibling_block(h):
         from_sibling(far, h).wait_recv()
         gather_math([block_sib(far)], h)
 
@@ -469,20 +470,28 @@
 
     for h in range(turns):
         start_gather(h)
+    gather_math([block_of(0)], first=True)
+    sibling_math(0)
     for d in range(1, far):
         for h in range(turns):
             step_gather(d, h)
+        gather_math([block_of(-d), block_of(d)])
+        sibling_math(d)
     wd_own.wait()
     wd_sib.wait()
-    end_gather(0)
-    hid_copy = share_hidden(0)
+    hid_copies = []
+    last_block(0)
+    last_block(1)
     for h in range(turns):
-        if h + 1 < turns:
-            end_gather(h + 1)
-        hid_copy.wait_recv()
-        start_scatter(h)
-        if h + 1 < turns:
-            hid_copy = share_hidden(h + 1)
+        last_sibling_block(h)
+        hid_copies.append(share_hidden(h))
+        if h + 2 < turns:
+            last_block(h + 2)
+        if h > 0:
+            hid_copies[h - 1].wait_recv()
+            start_scatter(h - 1)
+    hid_copies[turns - 1].wait_recv()
+    start_scatter(turns - 1)
     for t in range(1, far):
         for h in range(turns):
             step_scatter(t, h)

time: 80.3 us -> 77.5 us (0.965); the launches traced: 80.1 us -> 76 us
  Pallas kernels: 78.6 us -> 74.6 us
    pallas_call x1, Pallas kernels: 78.6 us -> 74.6 us  [body(): pl.pallas_call(functools.partial(kernel, cfg), out_shape=jax.ShapeDtypeSt...]
where the time goes in v3:
time: 77.5 us; the launch traced here: 76 us
  Pallas kernels  74.6 us (96%)
  local copies, waits for them, and re-layouts  1.45 us (2%)
    pallas_call x1, Pallas kernels, body(): pl.pallas_call(functools.partial(kernel, cfg), out_shape=jax.ShapeDtypeSt...  74.6 us

profile of v3, /device:TPU:1, one launch (start us, length us, event | category | flops | bytes accessed | tf_op | source)
XLA Modules:
  0.0 76.0 jit_solution(9522718462290267287)
XLA Ops:
  0.0 74.6 %shard_map.64 = bf16[224,128]{1,0:T(8,128)(2,1)} custom-call(bf16[224,128]{1,0:T(8,128)(2,1)} %bitcast.5, s32[2,128]{1,0:T(2,128)} %bitcast.7, bf16[64,224]{1,0:T(8,128)(2,1)} %bitcast.6, bf16[1,3584,128]{2,1,0:T(8,128)(2,1)} %wg_hbm.1, bf16[1,3584,128]{2,1,0:T(8,128)(2,1)} %wu_hbm.1, bf16[1,128,3584]{2,1,0:T(8,128)(2,1)} %wd_hbm.1), custom_call_target="tpu_custom_call" | custom-call | tf_op jit(solution)/shard_map/pallas_call | solution.py:596
  74.6 1.4 %copy.8 = bf16[128,224]{0,1:T(8,128)(2,1)} copy(bf16[128,224]{0,1:T(8,128)(2,1)} %bitcast.4) | data formatting | bytes 114688

commit v4 on v3

--- a/solution.py
+++ b/solution.py
@@ -419,8 +419,10 @@
             device_id_type=MESH,
         )
 
-    def add_and_pass(way, s, h, adds):
-        total = contribution((far - s) * (1 if way == 0 else -1), h)
+    def own_part(way, s, h):
+        return contribution((far - s) * (1 if way == 0 else -1), h)
+
+    def add_and_pass(way, s, h, adds, total):
         if adds:
             pass_on(way, s - 1, h).wait_recv()
             total = total + rsr[way, s - 1, h].astype(F32)
@@ -428,14 +430,18 @@
         go(pass_on(way, s, h))
 
     def start_scatter(h):
-        add_and_pass(h % 2, 0, h, False)
+        add_and_pass(h % 2, 0, h, False, own_part(h % 2, 0, h))
         if far > 1:
-            add_and_pass(1 - h % 2, 1, h, False)
-
-    def step_scatter(s, h):
-        add_and_pass(h % 2, s, h, True)
+            add_and_pass(1 - h % 2, 1, h, False, own_part(1 - h % 2, 1, h))
+
+    def own_parts(s, h):
+        late = own_part(1 - h % 2, s + 1, h) if s + 1 < far else None
+        return own_part(h % 2, s, h), late
+
+    def step_scatter(s, h, own):
+        add_and_pass(h % 2, s, h, True, own[0])
         if s + 1 < far:
-            add_and_pass(1 - h % 2, s + 1, h, True)
+            add_and_pass(1 - h % 2, s + 1, h, True, own[1])
 
     spread = (iota((hslots, half), 0) // SLOT) * cap + iota((hslots, half), 0) % SLOT
     unpick = jnp.where(
@@ -455,8 +461,7 @@
 
     own_back = pltpu.make_async_copy(ret_out.at[self_step], ret_in.at[me_e], ret_own)
 
-    def end_scatter(h):
-        total = contribution(0, h)
+    def end_scatter(h, total):
         for way in range(2):
             if far > 1 or h % 2 == way:
                 pass_on(way, far - 1, h).wait_recv()
@@ -493,10 +498,12 @@
     hid_copies[turns - 1].wait_recv()
     start_scatter(turns - 1)
     for t in range(1, far):
+        own = [own_parts(t, h) for h in range(turns)]
         for h in range(turns):
-            step_scatter(t, h)
+            step_scatter(t, h, own[h])
+    own = [contribution(0, h) for h in range(turns)]
     for h in range(turns):
-        end_scatter(h)
+        end_scatter(h, own[h])
 
     others = lg_recv.at[pl.ds(0, n_pipe - 1)]
     pltpu.make_async_copy(others, others, lg_rsem).wait()
@@ -516,7 +523,7 @@
     weighted = weighted * place[...]
     w_hi = weighted.astype(BF)
     w_lo = (weighted - w_hi.astype(F32)).astype(BF)
-    w_both = jnp.concatenate([w_hi, w_lo], axis=1)
+    w_both = jnp.concatenate([w_hi, w_lo], axis=1).T
 
     for copy in sent:
         copy.wait_send()
@@ -529,8 +536,8 @@
     back63 = ret_in.at[pl.ds(0, n_exp - 1)]
     pltpu.make_async_copy(back63, back63, ret_recv).wait()
     got = ret_in[...].reshape(slots, lanes)
-    both = dot(got, w_both, 0, 0)
-    out_ref[...] = (both[0:pw, 0:tok] + both[0:pw, tok : 2 * tok]).astype(BF)
+    both = dot(w_both, got)
+    out_ref[...] = (both[0:tok] + both[tok : 2 * tok]).T[0:pw, :].astype(BF)
     left63 = ret_out.at[pl.ds(0, n_exp - 1)]
     pltpu.make_async_copy(left63, left63, ret_send).wait()
 

time: 77.5 us -> 77.6 us (level)
  no operation moved by 1% of the time
where the time goes in v4:
time: 77.6 us; the launch traced here: 76 us
  Pallas kernels  74.6 us (96%)
  local copies, waits for them, and re-layouts  1.45 us (2%)
    pallas_call x1, Pallas kernels, body(): pl.pallas_call(functools.partial(kernel, cfg), out_shape=jax.ShapeDtypeSt...  74.6 us

profile of v4, /device:TPU:1, one launch (start us, length us, event | category | flops | bytes accessed | tf_op | source)
XLA Modules:
  0.0 76.0 jit_solution(16440571969440383311)
XLA Ops:
  0.0 74.6 %shard_map.64 = bf16[224,128]{1,0:T(8,128)(2,1)} custom-call(bf16[224,128]{1,0:T(8,128)(2,1)} %bitcast.5, s32[2,128]{1,0:T(2,128)} %bitcast.7, bf16[64,224]{1,0:T(8,128)(2,1)} %bitcast.6, bf16[1,3584,128]{2,1,0:T(8,128)(2,1)} %wg_hbm.1, bf16[1,3584,128]{2,1,0:T(8,128)(2,1)} %wu_hbm.1, bf16[1,128,3584]{2,1,0:T(8,128)(2,1)} %wd_hbm.1), custom_call_target="tpu_custom_call" | custom-call | tf_op jit(solution)/shard_map/pallas_call | solution.py:603
  74.6 1.4 %copy.8 = bf16[128,224]{0,1:T(8,128)(2,1)} copy(bf16[128,224]{0,1:T(8,128)(2,1)} %bitcast.4) | data formatting | bytes 114688
